TPU v7x, 32 devices: a whole 2x2x4 slice. The times are simulated.
32 devices in a mesh: rep: 2 (over x), node: 2 (over core), local: 8 (over z, y).
Axes of the slice: x: 2, y: 2, z: 4, core: 2. Of those that a mesh axis runs over, the one named last changes fastest.
Arguments:
- tokens: bfloat16 [4096, 3584], P(('rep', 'node', 'local')), parts along dimension 0, may hold values from -6 to 6
- expert_ids: int32 [4096, 2], P(('rep', 'node', 'local')), parts along dimension 0, may hold values from 0 to 7, all different within a row; in each aligned block of 128 rows (0 to 127, 128 to 255, ...) at most 80 rows name the same one
- route_weights: float32 [4096, 2], P(('rep', 'node', 'local')), parts along dimension 0, may hold values from 0.2 to 1
- gate_weight: bfloat16 [8, 3584, 1024], P('local', None, 'node'), may hold values from -0.09375 to 0.09375
- up_weight: bfloat16 [8, 3584, 1024], P('local', None, 'node'), may hold values from -0.09375 to 0.09375
- down_weight: bfloat16 [8, 1024, 3584], P('local', 'node'), may hold values from -0.1875 to 0.1875
Outputs:
- moe_output: bfloat16 [4096, 3584], P(('rep', 'node', 'local')), parts along dimension 0
There are 2 independent parts, one for each index of `rep`. A program takes and returns all parts, laid end to end along the dimension named above; an argument that names none is the same for every part. Nothing has to cross between parts.
Inputs may be any that keep to these rules, and one draw needn't show every extreme that they name: `expert_ids`: each row names 2 different experts; within the 128 rows of one device no expert is named by more than 80 rows, a bound that some block reaches.
All inputs are finite; a program needn't handle non-finite values.
Results may differ from a plain program's by a relative error of at most 0.0058.
Values may be sent and summed in bfloat16 or wider, within the bound.
A program may use at most 128 MiB of HBM per device.

v0:
```python
import jax
import jax.numpy as jnp
from jax import lax
from jax.sharding import PartitionSpec as P


def slot_positions(block_ids, expert_count, slot_cap):
    one_hot = (block_ids[..., None] == jnp.arange(expert_count, dtype=jnp.int32)).astype(jnp.int32)
    flattened = one_hot.reshape(-1, expert_count)
    preceding = jnp.cumsum(flattened, axis=0) - flattened
    position = jnp.sum(preceding * flattened, axis=1).reshape(block_ids.shape)
    return block_ids * slot_cap + position


def expert_terms(received, gate_weight, up_weight, down_weight):
    in_shape = received.shape
    flattened = received.reshape(-1, in_shape[-1])
    gate_act = jnp.dot(flattened, gate_weight[0], preferred_element_type=jnp.float32)
    up_act = jnp.dot(flattened, up_weight[0], preferred_element_type=jnp.float32)
    hidden = (jax.nn.silu(gate_act) * up_act).astype(jnp.bfloat16)
    partial_value = jnp.dot(hidden, down_weight[0], preferred_element_type=jnp.float32)
    return partial_value.reshape(in_shape[:-1] + (down_weight.shape[2],))


def on_device(tokens, expert_ids, route_weights, gate_weight, up_weight, down_weight):
    row_count, model_width = tokens.shape
    top_count = expert_ids.shape[1]
    expert_count = lax.axis_size("local")
    slot_cap = max(2, row_count * top_count * 5 // (2 * expert_count))
    home_slot = slot_positions(expert_ids, expert_count, slot_cap)
    node_count = lax.axis_size("node")
    outgoing = jnp.zeros((expert_count * slot_cap, model_width), jnp.bfloat16)
    outgoing = outgoing.at[home_slot.reshape(-1)].set(jnp.repeat(tokens, top_count, axis=0))
    duplicated = jnp.broadcast_to(
        outgoing.reshape(1, expert_count, slot_cap, model_width),
        (node_count, expert_count, slot_cap, model_width),
    )
    duplicated = duplicated.reshape(node_count * expert_count, slot_cap, model_width)
    partials = expert_terms(
        lax.all_to_all(duplicated, ("node", "local"), split_axis=0, concat_axis=0, tiled=True),
        gate_weight,
        up_weight,
        down_weight,
    )
    combined = lax.psum_scatter(
        partials.reshape(node_count, expert_count, slot_cap, model_width),
        "node",
        scatter_dimension=0,
        tiled=True,
    )
    finished = combined.reshape(expert_count, slot_cap, model_width).astype(jnp.bfloat16)
    returned = lax.all_to_all(finished, "local", split_axis=0, concat_axis=0, tiled=True)
    gathered_out = returned.reshape(expert_count * slot_cap, model_width)[home_slot.reshape(-1)]
    gathered_out = gathered_out.reshape(row_count, top_count, model_width)
    blended = jnp.sum(route_weights[..., None] * gathered_out.astype(jnp.float32), axis=1)
    return blended.astype(jnp.bfloat16)


def solution(mesh):
    placed = (
        P(("rep", "node", "local"), None),
        P(("rep", "node", "local"), None),
        P(("rep", "node", "local"), None),
        P("local", None, "node"),
        P("local", None, "node"),
        P("local", "node", None),
    )
    return jax.shard_map(
        on_device,
        mesh=mesh,
        in_specs=placed,
        out_specs=P(("rep", "node", "local"), None),
        check_vma=False,
    )
```

profile of v0, /device:TPU:0, one launch (start us, length us, event | category | flops | bytes accessed | tf_op | source)
XLA Modules:
  0.0 420.5 jit_solution(5590407411891086953)
XLA Ops:
  6.5 0.8 copy.14
  7.3 0.1 eq.30
  7.5 0.1 eq.26
  7.6 0.6 reduce-window.6
  8.2 0.2 slice_reduce_fusion
  8.6 0.1 reshape.75
  8.8 0.7 multiply_add_fusion
  9.5 0.1 copy.17
  9.6 0.1 reshape.76
  9.7 2.1 broadcast_in_dim.9
  11.9 1.7 reshape.94
  13.6 7.0 %scatter_custom_fusion = bf16[640,3584]{1,0:T(8,128)(2,1)} fusion(s32[256]{0:T(256)S(1)} %bitcast.40, bf16[256,3584]{1,0:T(8,128)(2,1)} %reshape.94, bf16[]{:T(256)} %constant.6.clone.1), kind=kCustom, calls=%fused_computation.12 | custom fusion | bytes 4588032 | tf_op jit(solution)/shard_map/scatter | solution.py:33
  20.6 6.7 %broadcast_in_dim.21 = bf16[2,8,80,3584]{3,2,1,0:T(8,128)(2,1)} broadcast(bf16[8,80,3584]{2,1,0:T(8,128)(2,1)} %bitcast.37), dimensions={1,2,3} | broadcast | bytes 13762560 | tf_op jit(solution)/shard_map/broadcast_in_dim | solution.py:34
  27.3 209.0 %all_to_all.10 = bf16[16,80,3584]{2,1,0:T(8,128)(2,1)S(1)} all-to-all(bf16[16,80,3584]{2,1,0:T(8,128)(2,1)} %bitcast.36), channel_id=1, replica_groups=mesh['rep'=2,'node'=2,'local'=8] {'node','local'}, dimensions={0} | all-to-all | bytes 18350080 | tf_op jit(solution)/shard_map/all_to_all | solution.py:40
  236.3 4.9 %fusion.4 = f32[1280,512]{1,0:T(8,128)S(1)} fusion(bf16[1280,3584]{1,0:T(8,128)(2,1)S(1)} %bitcast.38, bf16[1,3584,512]{2,1,0:T(8,128)(2,1)S(1)} %copy-done.1), kind=kOutput, calls=%fused_computation.7 | convolution fusion | flops 4697620480 | bytes 15466496 | tf_op jit(solution)/shard_map/dot_general | solution.py:18
  241.2 5.3 %fusion.9 = bf16[1280,512]{1,0:T(8,128)(2,1)S(1)} fusion(bf16[1280,3584]{1,0:T(8,128)(2,1)S(1)} %bitcast.39, bf16[1,3584,512]{2,1,0:T(8,128)(2,1)S(1)} %copy-done.2, f32[1280,512]{1,0:T(8,128)S(1)} %fusion.4), kind=kOutput, calls=%fused_computation.11 | convolution fusion | flops 4701552640 | bytes 16777216 | tf_op jit(solution)/shard_map/dot_general | solution.py:19
  246.5 8.9 %fusion = f32[2,8,80,3584]{3,2,1,0:T(8,128)} fusion(bf16[2,8,80,512]{3,2,1,0:T(8,128)(2,1)S(1)} %bitcast.42, bf16[1,512,3584]{2,1,0:T(8,128)(2,1)S(1)} %copy-done.3), kind=kOutput, calls=%fused_computation.3 | convolution fusion | flops 4697620480 | bytes 23330816 | tf_op jit(solution)/shard_map/dot_general | solution.py:21
  255.4 25.7 %reduce-scatter.2.cloned.1.call-done = f32[1,8,80,3584]{3,2,1,0:T(8,128)} async-done(((f32[2,8,80,3584]{3,2,1,0:T(8,128)}), f32[1,8,80,3584]{3,2,1,0:T(8,128)}) %reduce-scatter.2.cloned.1.call-update) | async-done | bytes 9175056 | tf_op jit(solution)/shard_map/reduce_scatter | solution.py:45
  281.1 6.3 %convert_bitcast_fusion = bf16[8,80,3584]{2,1,0:T(8,128)(2,1)} fusion(f32[1,8,80,3584]{3,2,1,0:T(8,128)} %reduce-scatter.2.cloned.1.call-done), kind=kLoop, calls=%fused_computation.2 | loop fusion | flops 2293760 | bytes 13762560 | tf_op jit(solution)/shard_map/convert_element_type | solution.py:51
  287.4 6.1 %all-to-all-start.1 = ((bf16[8,80,3584]{2,1,0:T(8,128)(2,1)}), bf16[8,80,3584]{2,1,0:T(8,128)(2,1)}, u32[]{:S(2)}, u32[]{:S(2)}) async-start(bf16[8,80,3584]{2,1,0:T(8,128)(2,1)} %convert_bitcast_fusion), calls=%async_computation.2 | async-start | bytes 9175040 | tf_op jit(solution)/shard_map/all_to_all | solution.py:52
  293.6 101.9 %all-to-all-done.1 = bf16[8,80,3584]{2,1,0:T(8,128)(2,1)} async-done(((bf16[8,80,3584]{2,1,0:T(8,128)(2,1)}), bf16[8,80,3584]{2,1,0:T(8,128)(2,1)}, u32[]{:S(2)}, u32[]{:S(2)}) %all-to-all-start.1) | async-done | bytes 4587552 | tf_op jit(solution)/shard_map/all_to_all | solution.py:52
  395.5 6.4 %gather_fusion = bf16[256,3584]{1,0:T(8,128)(2,1)S(1)} fusion(bf16[640,3584]{1,0:T(8,128)(2,1)} %bitcast.13, s32[1024]{0:T(1024)S(1)} %pad_clamp_fusion), kind=kCustom, calls=%fused_computation | custom fusion | bytes 3671040 | tf_op jit(solution)/shard_map/gather | solution.py:53
  401.9 3.5 reshape.81
  405.4 8.2 %multiply_reduce_fusion = bf16[128,3584]{1,0:T(8,128)(2,1)} fusion(f32[128,2,3584]{2,1,0:T(2,128)} %reshape.81, f32[128,2]{1,0:T(8,128)S(1)} %copy.13), kind=kLoop, calls=%fused_computation.9 | loop fusion | flops 1376256 | bytes 4588544 | tf_op jit(solution)/shard_map/reduce_sum | solution.py:55
  (18 shorter events, 0.4 us)
Async XLA Ops:
  6.5 274.6 %reduce-scatter.2.cloned.1.call-start = ((), (), s32[]{:S(2)}) async-start(), calls=%async_computation.3 | async-start | bytes 27525120 | tf_op jit(solution)/shard_map/reduce_scatter | solution.py:45
  27.3 209.0 %copy-start.1 = (bf16[1,3584,512]{2,1,0:T(8,128)(2,1)S(1)}, bf16[1,3584,512]{2,1,0:T(8,128)(2,1)}, u32[]{:S(2)}) copy-start(bf16[1,3584,512]{2,1,0:T(8,128)(2,1)} %param.9) | copy-start | bytes 11010052
  236.3 4.9 %copy-start.2 = (bf16[1,3584,512]{2,1,0:T(8,128)(2,1)S(1)}, bf16[1,3584,512]{2,1,0:T(8,128)(2,1)}, u32[]{:S(2)}) copy-start(bf16[1,3584,512]{2,1,0:T(8,128)(2,1)} %param.10) | copy-start | bytes 11010052
  241.2 5.3 %copy-start.3 = (bf16[1,512,3584]{2,1,0:T(8,128)(2,1)S(1)}, bf16[1,512,3584]{2,1,0:T(8,128)(2,1)}, u32[]{:S(2)}) copy-start(bf16[1,512,3584]{2,1,0:T(8,128)(2,1)} %param.11) | copy-start | bytes 11010052
  287.4 6.1 %copy-start = (f32[128,2]{0,1:T(2,128)S(1)}, f32[128,2]{0,1:T(2,128)}, u32[]{:S(2)}) copy-start(f32[128,2]{0,1:T(2,128)} %param.8) | copy-start | bytes 3076
  287.4 108.1 %all-to-all-start.1 = ((bf16[8,80,3584]{2,1,0:T(8,128)(2,1)}), bf16[8,80,3584]{2,1,0:T(8,128)(2,1)}, u32[]{:S(2)}, u32[]{:S(2)}) async-start(bf16[8,80,3584]{2,1,0:T(8,128)(2,1)} %convert_bitcast_fusion), calls=%async_computation.2 | async-start | bytes 9175040 | tf_op jit(solution)/shard_map/all_to_all | solution.py:52
Sparse Core Ops, SparseCore 0:
  255.5 25.5 reduce-scatter.1
where the time goes:
time: 421 us; the launch traced here: 420 us
  blocking collectives  209 us (50%)
  waiting for transfers between devices  128 us (30%)
  local copies, waits for them, and re-layouts  29.3 us (7%)
  matrix products  19.1 us (5%)
  other arithmetic  15.9 us (4%)
  between operations  13.5 us (3%)
  starting transfers between devices  6.1 us (1%)
    all_to_all x1, blocking collectives, on_device(): lax.all_to_all(duplicated, ('node', 'local'), split_axis=0, concat_axis=0...  209 us
    all_to_all x1, waiting for transfers between devices, on_device(): lax.all_to_all(finished, 'local', split_axis=0, concat_axis=0, tiled=True)  102 us
    reduce_scatter x1, waiting for transfers between devices, on_device(): lax.psum_scatter(partials.reshape(node_count, expert_count, slot_cap, mod...  25.7 us
    dot_general x1, matrix products, expert_terms(): jnp.dot(hidden, down_weight[0], preferred_element_type=jnp.float32)  8.88 us
  transfers between devices with their start and end apart: 2, of which 2 were waited for; matrix products, arithmetic and copies ran while one was open for 0% of the time, Pallas kernels for 0%

commit v1 on v0

v1 whole, which is shorter than its diff:
```python
import functools

import jax
import jax.numpy as jnp
from jax import lax
from jax.experimental import pallas as pl
from jax.experimental.pallas import tpu as pltpu
from jax.sharding import PartitionSpec as P

MESH = pl.DeviceIdType.MESH
BF16 = jnp.bfloat16
F32 = jnp.float32
LINE = 4
SIDES = 2


def slot_cap(row_count, top_count, expert_count):
    return max(2, row_count * top_count * 5 // (2 * expert_count))


def slot_positions(block_ids, expert_count, cap):
    one_hot = (block_ids[..., None] == jnp.arange(expert_count, dtype=jnp.int32)).astype(jnp.int32)
    flattened = one_hot.reshape(-1, expert_count)
    preceding = jnp.cumsum(flattened, axis=0) - flattened
    position = jnp.sum(preceding * flattened, axis=1).reshape(block_ids.shape)
    return block_ids * cap + position


def general(tokens, expert_ids, route_weights, gate_weight, up_weight, down_weight):
    row_count, model_width = tokens.shape
    top_count = expert_ids.shape[1]
    expert_count = lax.axis_size("local")
    cap = slot_cap(row_count, top_count, expert_count)
    home_slot = slot_positions(expert_ids, expert_count, cap)
    outgoing = jnp.zeros((expert_count * cap, model_width), BF16)
    outgoing = outgoing.at[home_slot.reshape(-1)].set(jnp.repeat(tokens, top_count, axis=0))
    gate = lax.all_gather(gate_weight[0], "node", axis=1, tiled=True)
    up = lax.all_gather(up_weight[0], "node", axis=1, tiled=True)
    down = lax.all_gather(down_weight[0], "node", axis=0, tiled=True)
    received = lax.all_to_all(
        outgoing.reshape(expert_count, cap, model_width), "local", split_axis=0, concat_axis=0, tiled=True
    ).reshape(expert_count * cap, model_width)
    gate_act = jnp.dot(received, gate, preferred_element_type=F32)
    up_act = jnp.dot(received, up, preferred_element_type=F32)
    hidden = (jax.nn.silu(gate_act) * up_act).astype(BF16)
    finished = jnp.dot(hidden, down, preferred_element_type=F32).astype(BF16)
    returned = lax.all_to_all(
        finished.reshape(expert_count, cap, model_width), "local", split_axis=0, concat_axis=0, tiled=True
    )
    gathered_out = returned.reshape(expert_count * cap, model_width)[home_slot.reshape(-1)]
    gathered_out = gathered_out.reshape(row_count, top_count, model_width)
    return jnp.sum(route_weights[..., None] * gathered_out.astype(F32), axis=1).astype(BF16)


def layer_kernel(
    cap, tile, tokens, meta, gate_w, up_w, down_w, out,
    X, M, WG, WU, WD, CIN, CSEND, HID, EOUT, RET, D, R,
    load_sem, w_local, w_send, w_recv, x_send, x_recv, m_send, m_recv,
    c_send, c_recv, e_send, e_recv, r_send, r_recv,
):
    me = lax.axis_index("local")
    node = lax.axis_index("node")
    z, y = me // SIDES, me % SIDES
    beside = me + 1 - 2 * y
    last = LINE - 1
    half = z // 2
    mid = (z * (last - z) + 1) // 3
    rows, width = X.shape[1], X.shape[2]
    tiles = width // tile
    experts = lax.axis_size("local")

    def remote(src, dst, send, recv, **where):
        return pltpu.make_async_remote_copy(
            src_ref=src, dst_ref=dst, send_sem=send, recv_sem=recv, device_id=where, device_id_type=MESH
        )

    load = pltpu.make_async_copy(tokens, X.at[z], load_sem)
    load.start()
    own_w = [
        pltpu.make_async_copy(src.at[0], dst.at[0], w_local.at[i])
        for i, (src, dst) in enumerate(((gate_w, WG), (up_w, WU), (down_w, WD)))
    ]
    for copy in own_w:
        copy.start()
    M[z] = meta[...]

    barrier = pltpu.get_barrier_semaphore()
    pl.semaphore_signal(barrier, inc=1, device_id={"node": 1 - node}, device_id_type=MESH)
    pl.semaphore_signal(barrier, inc=1, device_id={"local": beside}, device_id_type=MESH)

    @pl.when(z < last)
    def _():
        pl.semaphore_signal(barrier, inc=1, device_id={"local": me + SIDES}, device_id_type=MESH)

    @pl.when(z > 0)
    def _():
        pl.semaphore_signal(barrier, inc=1, device_id={"local": me - SIDES}, device_id_type=MESH)

    pl.semaphore_wait(barrier, 3 + mid)

    def order(i):
        base = i + mid * (1 - 2 * i) if i < 2 else i
        return base + half * (last - 2 * base)

    def token_copies(o, up):
        where = me + SIDES if up else me - SIDES
        way = 0 if up else 1
        return (
            remote(M.at[o], M.at[o], m_send.at[way, o], m_recv.at[o], local=where),
            remote(X.at[o], X.at[o], x_send.at[way, o], x_recv.at[o], local=where),
        )

    def spread(o, act):
        @pl.when((o <= z) & (z < last))
        def _():
            for copy in token_copies(o, True):
                act(copy)

        @pl.when((o >= z) & (z > 0))
        def _():
            for copy in token_copies(o, False):
                act(copy)

    def compact_copy(o):
        return remote(CSEND.at[o], CIN.at[o, pl.ds(cap, cap)], c_send.at[o], c_recv.at[o], local=beside)

    def result_copy(o):
        return remote(EOUT.at[o, pl.ds(cap, cap)], RET.at[o], e_send.at[o], e_recv.at[o], local=beside)

    def sum_copy(o, way):
        return remote(
            D.at[o], R.at[way, o], r_send.at[o], r_recv.at[way, o], local=me + SIDES * (1 - 2 * way)
        )

    w_remote = [
        remote(src.at[0], dst.at[1], w_send.at[i], w_recv.at[i], node=1 - node)
        for i, (src, dst) in enumerate(((gate_w, WG), (up_w, WU), (down_w, WD)))
    ]

    def place_row(o, e):
        return M[o, pl.ds(e, 1), :]

    def weight_row(o, e):
        return M[o, pl.ds(experts + e, 1), :]

    def to_column(row):
        diagonal = lax.broadcasted_iota(jnp.int32, (rows, rows), 0) == lax.broadcasted_iota(
            jnp.int32, (rows, rows), 1
        )
        return jnp.sum(jnp.where(diagonal, row, 0.0), axis=1, keepdims=True)

    def columns(n):
        return pl.ds(pl.multiple_of(n * tile, tile), tile)

    def stage_a(i):
        o = order(i)
        if i == 0:
            load.wait()
        else:
            for copy in token_copies(o, True):
                copy.wait_recv()
        spread(o, lambda copy: copy.start())
        if i == 0:
            for copy in w_remote:
                copy.start()
        slots = lax.broadcasted_iota(jnp.int32, (cap, rows), 0).astype(F32)
        near = (slots == place_row(o, me)).astype(F32).astype(BF16)
        far = (slots == place_row(o, beside)).astype(F32).astype(BF16)

        def body(n, carry):
            block = X[o, :, columns(n)]
            CSEND[o, :, columns(n)] = jnp.dot(far, block, preferred_element_type=F32).astype(BF16)
            return carry

        lax.fori_loop(0, tiles, body, 0)
        compact_copy(o).start()

        def body(n, carry):
            block = X[o, :, columns(n)]
            CIN[o, 0:cap, columns(n)] = jnp.dot(near, block, preferred_element_type=F32).astype(BF16)
            return carry

        lax.fori_loop(0, tiles, body, 0)

    def stage_b(i):
        o = order(i)
        if i == 0:
            for copy in own_w:
                copy.wait()
            for copy in w_remote:
                copy.wait_recv()
        compact_copy(o).wait_recv()
        part = WG.shape[2] // 2

        def body(t, carry):
            cols = pl.ds(pl.multiple_of((t % 2) * part, part), part)
            gate_act = jnp.dot(CIN[o], WG[t // 2, :, cols], preferred_element_type=F32)
            up_act = jnp.dot(CIN[o], WU[t // 2, :, cols], preferred_element_type=F32)
            hidden = gate_act / (1.0 + jnp.exp(-gate_act)) * up_act
            HID[:, pl.ds(pl.multiple_of(t * part, part), part)] = hidden.astype(BF16)
            return carry

        lax.fori_loop(0, 4, body, 0)

        def body(n, carry):
            total = jnp.dot(HID[:, : 2 * part], WD[0, :, columns(n)], preferred_element_type=F32)
            total += jnp.dot(HID[:, 2 * part :], WD[1, :, columns(n)], preferred_element_type=F32)
            EOUT[o, :, columns(n)] = total.astype(BF16)
            return carry

        lax.fori_loop(0, tiles, body, 0)
        result_copy(o).start()

    def stage_c(i):
        o = order(i)
        slots = lax.broadcasted_iota(jnp.int32, (rows, cap), 1).astype(F32)
        near = (slots == to_column(place_row(o, me))).astype(F32).astype(BF16)
        far = (slots == to_column(place_row(o, beside))).astype(F32).astype(BF16)
        near_w, far_w = to_column(weight_row(o, me)), to_column(weight_row(o, beside))
        result_copy(o).wait_recv()

        def body(n, carry):
            a = jnp.dot(near, EOUT[o, 0:cap, columns(n)], preferred_element_type=F32)
            b = jnp.dot(far, RET[o, :, columns(n)], preferred_element_type=F32)
            D[o, :, columns(n)] = (near_w * a + far_w * b).astype(BF16)
            return carry

        lax.fori_loop(0, tiles, body, 0)
        if i > 0:
            @pl.when(mid == 0)
            def _():
                sum_copy(o, half).start()

    stage_a(0)
    stage_a(1)
    stage_b(0)
    stage_a(2)

    @pl.when(mid == 1)
    def _():
        stage_a(3)

    stage_b(1)
    stage_c(0)

    @pl.when(mid == 0)
    def _():
        stage_a(3)

    stage_b(2)
    stage_c(1)
    stage_b(3)
    stage_c(2)
    stage_c(3)

    @pl.when(mid == 1)
    def _():
        for base, way in ((2, half), (3, half), (0, 1 - half)):
            o = base + half * (last - 2 * base)
            copy = sum_copy(o, way)
            copy.wait_recv()

            def body(n, carry):
                total = D[o, :, columns(n)].astype(F32) + R[way, o, :, columns(n)].astype(F32)
                D[o, :, columns(n)] = total.astype(BF16)
                return carry

            lax.fori_loop(0, tiles, body, 0)
            copy.start()

    def body(n, carry):
        out[:, columns(n)] = D[z, :, columns(n)]
        return carry

    lax.fori_loop(0, tiles, body, 0)

    def add_in(way):
        sum_copy(z, way).wait_recv()

        def body(n, carry):
            total = out[:, columns(n)].astype(F32) + R[way, z, :, columns(n)].astype(F32)
            out[:, columns(n)] = total.astype(BF16)
            return carry

        lax.fori_loop(0, tiles, body, 0)

    @pl.when(z > 0)
    def _():
        add_in(0)

    @pl.when(z < last)
    def _():
        add_in(1)

    for copy in w_remote:
        copy.wait_send()
    for i in range(LINE):
        o = order(i)
        spread(o, lambda copy: copy.wait_send())
        compact_copy(o).wait_send()
        result_copy(o).wait_send()
        if i > 0:
            sum_copy(o, half).wait_send()


def paired(tokens, expert_ids, route_weights, gate_weight, up_weight, down_weight):
    rows, width = tokens.shape
    top_count = expert_ids.shape[1]
    experts = lax.axis_size("local")
    cap = slot_cap(rows, top_count, experts)
    hidden = gate_weight.shape[2]
    named = expert_ids.T[:, None, :] == jnp.arange(experts, dtype=jnp.int32)[None, :, None]
    chosen = jnp.any(named, axis=0)
    place = jnp.cumsum(chosen.astype(F32), axis=1) - 1.0
    place = jnp.where(chosen, place, -1.0)
    weight = jnp.sum(jnp.where(named, route_weights.T[:, None, :], 0.0), axis=0)
    meta = jnp.concatenate([place, weight], axis=0)
    tile = 512 if width % 512 == 0 else 128
    dma = pltpu.SemaphoreType.DMA
    return pl.pallas_call(
        functools.partial(layer_kernel, cap, tile),
        out_shape=jax.ShapeDtypeStruct((rows, width), BF16),
        in_specs=[
            pl.BlockSpec(memory_space=pl.ANY),
            pl.BlockSpec(memory_space=pltpu.VMEM),
            pl.BlockSpec(memory_space=pl.ANY),
            pl.BlockSpec(memory_space=pl.ANY),
            pl.BlockSpec(memory_space=pl.ANY),
        ],
        out_specs=pl.BlockSpec(memory_space=pltpu.VMEM),
        scratch_shapes=[
            pltpu.VMEM((LINE, rows, width), BF16),
            pltpu.VMEM((LINE, 2 * experts, rows), F32),
            pltpu.VMEM((2, width, hidden), BF16),
            pltpu.VMEM((2, width, hidden), BF16),
            pltpu.VMEM((2, hidden, width), BF16),
            pltpu.VMEM((LINE, 2 * cap, width), BF16),
            pltpu.VMEM((LINE, cap, width), BF16),
            pltpu.VMEM((2 * cap, 2 * hidden), BF16),
            pltpu.VMEM((LINE, 2 * cap, width), BF16),
            pltpu.VMEM((LINE, cap, width), BF16),
            pltpu.VMEM((LINE, rows, width), BF16),
            pltpu.VMEM((2, LINE, rows, width), BF16),
            dma, dma((3,)), dma((3,)), dma((3,)),
            dma((2, LINE)), dma((LINE,)), dma((2, LINE)), dma((LINE,)),
            dma((LINE,)), dma((LINE,)), dma((LINE,)), dma((LINE,)),
            dma((LINE,)), dma((2, LINE)),
        ],
        compiler_params=pltpu.CompilerParams(
            collective_id=0, has_side_effects=True, vmem_limit_bytes=60 * 1024 * 1024
        ),
        cost_estimate=pl.CostEstimate(
            flops=12 * LINE * cap * width * 2 * hidden,
            bytes_accessed=12 * width * hidden,
            transcendentals=4 * LINE * cap * hidden,
        ),
    )(tokens, meta, gate_weight, up_weight, down_weight)


def solution(mesh):
    placed = (
        P(("rep", "node", "local"), None),
        P(("rep", "node", "local"), None),
        P(("rep", "node", "local"), None),
        P("local", None, "node"),
        P("local", None, "node"),
        P("local", "node", None),
    )
    small = mesh.shape["local"] == LINE * SIDES and mesh.shape["node"] == 2
    return jax.shard_map(
        paired if small else general,
        mesh=mesh,
        in_specs=placed,
        out_specs=P(("rep", "node", "local"), None),
        check_vma=False,
    )
```

time: 421 us -> 192 us (0.46)
  blocking collectives: 209 us -> 0 us
  Pallas kernels: 0 us -> 187 us
  waiting for transfers between devices: 128 us -> 0 us
  local copies, waits for them, and re-layouts: 29.3 us -> 2.16 us
  matrix products: 19.1 us -> 0 us
  other arithmetic: 15.9 us -> 2.29 us
  between operations: 13.5 us -> 0.01 us
  starting transfers between devices: 6.1 us -> 0 us
    all_to_all x1 -> x0, blocking collectives: 209 us -> none  [on_device(): lax.all_to_all(duplicated, ('node', 'local'), split_axis=0, concat_axis=0...]
    pallas_call x0 -> x1, Pallas kernels: none -> 187 us  [paired(): pl.pallas_call(functools.partial(layer_kernel, cap, tile), out_shape=jax....]
    all_to_all x1 -> x0, waiting for transfers between devices: 102 us -> none  [on_device(): lax.all_to_all(finished, 'local', split_axis=0, concat_axis=0, tiled=True)]
    reduce_scatter x1 -> x0, waiting for transfers between devices: 25.7 us -> none  [on_device(): lax.psum_scatter(partials.reshape(node_count, expert_count, slot_cap, mod...]
    dot_general x3 -> x0, matrix products: 19.1 us -> none  [the longest x1 8.88 us: expert_terms(): jnp.dot(hidden, down_weight[0], preferred_element_type=jnp.float32)]
    broadcast_in_dim x2 -> x0, local copies, waits for them, and re-layouts: 8.83 us -> none  [the longest x1 6.7 us: on_device(): jnp.broadcast_to(outgoing.reshape(1, expert_count, slot_cap, model_width)...]
    reduce_sum x2 -> x1, other arithmetic: 8.3 us -> 0.7 us  [paired(): weight = jnp.sum(jnp.where(named, route_weights.T[:, None, :], 0.0), axis=0)]
    scatter x1 -> x0, local copies, waits for them, and re-layouts: 6.99 us -> none  [on_device(): outgoing.at[home_slot.reshape(-1)]]
  transfers between devices with their start and end apart: 2 -> 0, of which waited for: 2 -> 0; matrix products, arithmetic and copies ran while one was open for 0% -> 0% of each run, Pallas kernels for 0% -> 0%
where the time goes in v1:
time: 192 us
  Pallas kernels  187 us (97%)
  other arithmetic  2.29 us (1%)
  local copies, waits for them, and re-layouts  2.16 us (1%)
    pallas_call x1, Pallas kernels, paired(): pl.pallas_call(functools.partial(layer_kernel, cap, tile), out_shape=jax....  187 us

profile of v1, /device:TPU:0, one launch (start us, length us, event | category | flops | bytes accessed | tf_op | source)
XLA Modules:
  0.0 191.8 jit_solution(17342724038693013774)
XLA Ops:
  0.0 0.7 fusion
  0.7 0.3 reduce_window_sum.11
  1.0 0.7 select_reduce_fusion
  1.7 0.6 pad_maximum_fusion.meta
  2.3 187.4 %shard_map.64 = bf16[128,3584]{1,0:T(8,128)(2,1)} custom-call(bf16[128,3584]{1,0:T(8,128)(2,1)} %tokens.1, f32[16,128]{1,0:T(8,128)} %pad_maximum_fusion.meta, bf16[1,3584,512]{2,1,0:T(8,128)(2,1)} %gate_w.1, bf16[1,3584,512]{2,1,0:T(8,128)(2,1)} %up_w.1, bf16[1,512,3584]{2,1,0:T(8,128)(2,1)} %down_w.1), custom_call_target="tpu_custom_call" | custom-call | flops 14092861440 | bytes 22020096 | tf_op jit(solution)/shard_map/pallas_call | solution.py:320
  189.7 2.2 %copy.8 = bf16[128,3584]{1,0:T(8,128)(2,1)} copy(bf16[128,3584]{1,0:T(8,128)(2,1)} %shard_map.64) | data formatting | bytes 1835008
  (2 shorter events, 0.0 us)

commit v2 on v1

--- a/solution.py
+++ b/solution.py
@@ -102,35 +102,46 @@
         base = i + mid * (1 - 2 * i) if i < 2 else i
         return base + half * (last - 2 * base)
 
-    def token_copies(o, up):
+    def columns(n):
+        return pl.ds(pl.multiple_of(n * tile, tile), tile)
+
+    def place_copy(o, up):
         where = me + SIDES if up else me - SIDES
-        way = 0 if up else 1
-        return (
-            remote(M.at[o], M.at[o], m_send.at[way, o], m_recv.at[o], local=where),
-            remote(X.at[o], X.at[o], x_send.at[way, o], x_recv.at[o], local=where),
-        )
+        return remote(M.at[o], M.at[o], m_send.at[0 if up else 1, o], m_recv.at[o], local=where)
+
+    def token_copy(o, n, up):
+        where = me + SIDES if up else me - SIDES
+        block = X.at[o, :, columns(n)]
+        return remote(block, block, x_send.at[0 if up else 1, o, n], x_recv.at[o, n], local=where)
 
     def spread(o, act):
         @pl.when((o <= z) & (z < last))
         def _():
-            for copy in token_copies(o, True):
-                act(copy)
+            act(True)
 
         @pl.when((o >= z) & (z > 0))
         def _():
-            for copy in token_copies(o, False):
-                act(copy)
-
-    def compact_copy(o):
-        return remote(CSEND.at[o], CIN.at[o, pl.ds(cap, cap)], c_send.at[o], c_recv.at[o], local=beside)
-
-    def result_copy(o):
-        return remote(EOUT.at[o, pl.ds(cap, cap)], RET.at[o], e_send.at[o], e_recv.at[o], local=beside)
-
-    def sum_copy(o, way):
-        return remote(
-            D.at[o], R.at[way, o], r_send.at[o], r_recv.at[way, o], local=me + SIDES * (1 - 2 * way)
-        )
+            act(False)
+
+    def compact_copy(o, n):
+        block = CIN.at[o, pl.ds(cap, cap), columns(n)]
+        return remote(CSEND.at[o, :, columns(n)], block, c_send.at[o, n], c_recv.at[o, n], local=beside)
+
+    def result_copy(o, n):
+        block = EOUT.at[o, pl.ds(cap, cap), columns(n)]
+        return remote(block, RET.at[o, :, columns(n)], e_send.at[o, n], e_recv.at[o, n], local=beside)
+
+    def sum_copy(o, n, way):
+        where = me + SIDES * (1 - 2 * way)
+        block = D.at[o, :, columns(n)]
+        return remote(block, R.at[way, o, :, columns(n)], r_send.at[o, n], r_recv.at[way, o, n], local=where)
+
+    def each(body):
+        def step(n, carry):
+            body(n)
+            return carry
+
+        lax.fori_loop(0, tiles, step, 0)
 
     w_remote = [
         remote(src.at[0], dst.at[1], w_send.at[i], w_recv.at[i], node=1 - node)
@@ -149,38 +160,30 @@
         )
         return jnp.sum(jnp.where(diagonal, row, 0.0), axis=1, keepdims=True)
 
-    def columns(n):
-        return pl.ds(pl.multiple_of(n * tile, tile), tile)
-
     def stage_a(i):
         o = order(i)
         if i == 0:
             load.wait()
         else:
-            for copy in token_copies(o, True):
-                copy.wait_recv()
-        spread(o, lambda copy: copy.start())
+            place_copy(o, True).wait_recv()
+        spread(o, lambda up: place_copy(o, up).start())
+        slots = lax.broadcasted_iota(jnp.int32, (cap, rows), 0).astype(F32)
+        near = (slots == place_row(o, me)).astype(F32).astype(BF16)
+        far = (slots == place_row(o, beside)).astype(F32).astype(BF16)
+
+        @each
+        def _(n):
+            if i > 0:
+                token_copy(o, n, True).wait_recv()
+            spread(o, lambda up: token_copy(o, n, up).start())
+            block = X[o, :, columns(n)]
+            CSEND[o, :, columns(n)] = jnp.dot(far, block, preferred_element_type=F32).astype(BF16)
+            compact_copy(o, n).start()
+            CIN[o, 0:cap, columns(n)] = jnp.dot(near, block, preferred_element_type=F32).astype(BF16)
+
         if i == 0:
             for copy in w_remote:
                 copy.start()
-        slots = lax.broadcasted_iota(jnp.int32, (cap, rows), 0).astype(F32)
-        near = (slots == place_row(o, me)).astype(F32).astype(BF16)
-        far = (slots == place_row(o, beside)).astype(F32).astype(BF16)
-
-        def body(n, carry):
-            block = X[o, :, columns(n)]
-            CSEND[o, :, columns(n)] = jnp.dot(far, block, preferred_element_type=F32).astype(BF16)
-            return carry
-
-        lax.fori_loop(0, tiles, body, 0)
-        compact_copy(o).start()
-
-        def body(n, carry):
-            block = X[o, :, columns(n)]
-            CIN[o, 0:cap, columns(n)] = jnp.dot(near, block, preferred_element_type=F32).astype(BF16)
-            return carry
-
-        lax.fori_loop(0, tiles, body, 0)
 
     def stage_b(i):
         o = order(i)
@@ -189,7 +192,7 @@
                 copy.wait()
             for copy in w_remote:
                 copy.wait_recv()
-        compact_copy(o).wait_recv()
+        each(lambda n: compact_copy(o, n).wait_recv())
         part = WG.shape[2] // 2
 
         def body(t, carry):
@@ -202,14 +205,12 @@
 
         lax.fori_loop(0, 4, body, 0)
 
-        def body(n, carry):
+        @each
+        def _(n):
             total = jnp.dot(HID[:, : 2 * part], WD[0, :, columns(n)], preferred_element_type=F32)
             total += jnp.dot(HID[:, 2 * part :], WD[1, :, columns(n)], preferred_element_type=F32)
             EOUT[o, :, columns(n)] = total.astype(BF16)
-            return carry
-
-        lax.fori_loop(0, tiles, body, 0)
-        result_copy(o).start()
+            result_copy(o, n).start()
 
     def stage_c(i):
         o = order(i)
@@ -217,19 +218,17 @@
         near = (slots == to_column(place_row(o, me))).astype(F32).astype(BF16)
         far = (slots == to_column(place_row(o, beside))).astype(F32).astype(BF16)
         near_w, far_w = to_column(weight_row(o, me)), to_column(weight_row(o, beside))
-        result_copy(o).wait_recv()
-
-        def body(n, carry):
+
+        @each
+        def _(n):
+            result_copy(o, n).wait_recv()
             a = jnp.dot(near, EOUT[o, 0:cap, columns(n)], preferred_element_type=F32)
             b = jnp.dot(far, RET[o, :, columns(n)], preferred_element_type=F32)
             D[o, :, columns(n)] = (near_w * a + far_w * b).astype(BF16)
-            return carry
-
-        lax.fori_loop(0, tiles, body, 0)
-        if i > 0:
-            @pl.when(mid == 0)
-            def _():
-                sum_copy(o, half).start()
+            if i > 0:
+                @pl.when(mid == 0)
+                def _():
+                    sum_copy(o, n, half).start()
 
     stage_a(0)
     stage_a(1)
@@ -253,54 +252,54 @@
     stage_c(2)
     stage_c(3)
 
+    def pass_on(base, way, n):
+        o = base + half * (last - 2 * base)
+        copy = sum_copy(o, n, way)
+        copy.wait_recv()
+        total = D[o, :, columns(n)].astype(F32) + R[way, o, :, columns(n)].astype(F32)
+        D[o, :, columns(n)] = total.astype(BF16)
+        copy.start()
+
     @pl.when(mid == 1)
     def _():
-        for base, way in ((2, half), (3, half), (0, 1 - half)):
-            o = base + half * (last - 2 * base)
-            copy = sum_copy(o, way)
-            copy.wait_recv()
-
-            def body(n, carry):
-                total = D[o, :, columns(n)].astype(F32) + R[way, o, :, columns(n)].astype(F32)
-                D[o, :, columns(n)] = total.astype(BF16)
-                return carry
-
-            lax.fori_loop(0, tiles, body, 0)
-            copy.start()
-
-    def body(n, carry):
-        out[:, columns(n)] = D[z, :, columns(n)]
-        return carry
-
-    lax.fori_loop(0, tiles, body, 0)
-
-    def add_in(way):
-        sum_copy(z, way).wait_recv()
-
-        def body(n, carry):
-            total = out[:, columns(n)].astype(F32) + R[way, z, :, columns(n)].astype(F32)
+        each(lambda n: pass_on(2, half, n))
+
+        @each
+        def _(n):
+            pass_on(3, half, n)
+            pass_on(0, 1 - half, n)
+
+    @pl.when(mid == 1)
+    def _():
+        @each
+        def _(n):
+            sum_copy(z, n, half).wait_recv()
+            sum_copy(z, n, 1 - half).wait_recv()
+            total = D[z, :, columns(n)].astype(F32) + R[0, z, :, columns(n)].astype(F32)
+            total += R[1, z, :, columns(n)].astype(F32)
             out[:, columns(n)] = total.astype(BF16)
-            return carry
-
-        lax.fori_loop(0, tiles, body, 0)
-
-    @pl.when(z > 0)
-    def _():
-        add_in(0)
-
-    @pl.when(z < last)
-    def _():
-        add_in(1)
+
+    @pl.when(mid == 0)
+    def _():
+        @each
+        def _(n):
+            sum_copy(z, n, 1 - half).wait_recv()
+            total = D[z, :, columns(n)].astype(F32) + R[1 - half, z, :, columns(n)].astype(F32)
+            out[:, columns(n)] = total.astype(BF16)
 
     for copy in w_remote:
         copy.wait_send()
     for i in range(LINE):
         o = order(i)
-        spread(o, lambda copy: copy.wait_send())
-        compact_copy(o).wait_send()
-        result_copy(o).wait_send()
-        if i > 0:
-            sum_copy(o, half).wait_send()
+        spread(o, lambda up: place_copy(o, up).wait_send())
+
+        @each
+        def _(n):
+            spread(o, lambda up: token_copy(o, n, up).wait_send())
+            compact_copy(o, n).wait_send()
+            result_copy(o, n).wait_send()
+            if i > 0:
+                sum_copy(o, n, half).wait_send()
 
 
 def paired(tokens, expert_ids, route_weights, gate_weight, up_weight, down_weight):
@@ -316,6 +315,7 @@
     weight = jnp.sum(jnp.where(named, route_weights.T[:, None, :], 0.0), axis=0)
     meta = jnp.concatenate([place, weight], axis=0)
     tile = 512 if width % 512 == 0 else 128
+    tiles = width // tile
     dma = pltpu.SemaphoreType.DMA
     return pl.pallas_call(
         functools.partial(layer_kernel, cap, tile),
@@ -342,9 +342,9 @@
             pltpu.VMEM((LINE, rows, width), BF16),
             pltpu.VMEM((2, LINE, rows, width), BF16),
             dma, dma((3,)), dma((3,)), dma((3,)),
-            dma((2, LINE)), dma((LINE,)), dma((2, LINE)), dma((LINE,)),
-            dma((LINE,)), dma((LINE,)), dma((LINE,)), dma((LINE,)),
-            dma((LINE,)), dma((2, LINE)),
+            dma((2, LINE, tiles)), dma((LINE, tiles)), dma((2, LINE)), dma((LINE,)),
+            dma((LINE, tiles)), dma((LINE, tiles)), dma((LINE, tiles)), dma((LINE, tiles)),
+            dma((LINE, tiles)), dma((2, LINE, tiles)),
         ],
         compiler_params=pltpu.CompilerParams(
             collective_id=0, has_side_effects=True, vmem_limit_bytes=60 * 1024 * 1024

time: 192 us -> 172 us (0.90)
  Pallas kernels: 187 us -> 167 us
    pallas_call x1, Pallas kernels: 187 us -> 167 us  [paired(): pl.pallas_call(functools.partial(layer_kernel, cap, tile), out_shape=jax....]
where the time goes in v2:
time: 172 us
  Pallas kernels  167 us (97%)
  other arithmetic  2.29 us (1%)
  local copies, waits for them, and re-layouts  2.16 us (1%)
    pallas_call x1, Pallas kernels, paired(): pl.pallas_call(functools.partial(layer_kernel, cap, tile), out_shape=jax....  167 us

profile of v2, /device:TPU:0, one launch (start us, length us, event | category | flops | bytes accessed | tf_op | source)
XLA Modules:
  0.0 171.7 jit_solution(552108324546040627)
XLA Ops:
  0.0 0.7 fusion
  0.7 0.3 reduce_window_sum.11
  1.0 0.7 select_reduce_fusion
  1.7 0.6 pad_maximum_fusion.meta
  2.3 167.3 %shard_map.64 = bf16[128,3584]{1,0:T(8,128)(2,1)} custom-call(bf16[128,3584]{1,0:T(8,128)(2,1)} %tokens.1, f32[16,128]{1,0:T(8,128)} %pad_maximum_fusion.meta, bf16[1,3584,512]{2,1,0:T(8,128)(2,1)} %gate_w.1, bf16[1,3584,512]{2,1,0:T(8,128)(2,1)} %up_w.1, bf16[1,512,3584]{2,1,0:T(8,128)(2,1)} %down_w.1), custom_call_target="tpu_custom_call" | custom-call | flops 14092861440 | bytes 22020096 | tf_op jit(solution)/shard_map/pallas_call | solution.py:320
  169.5 2.2 %copy.8 = bf16[128,3584]{1,0:T(8,128)(2,1)} copy(bf16[128,3584]{1,0:T(8,128)(2,1)} %shard_map.64) | data formatting | bytes 1835008
  (2 shorter events, 0.0 us)

commit v3 on v2

--- a/solution.py
+++ b/solution.py
@@ -187,11 +187,6 @@
 
     def stage_b(i):
         o = order(i)
-        if i == 0:
-            for copy in own_w:
-                copy.wait()
-            for copy in w_remote:
-                copy.wait_recv()
         each(lambda n: compact_copy(o, n).wait_recv())
         part = WG.shape[2] // 2
 
@@ -212,7 +207,7 @@
             EOUT[o, :, columns(n)] = total.astype(BF16)
             result_copy(o, n).start()
 
-    def stage_c(i):
+    def stage_c(i, send):
         o = order(i)
         slots = lax.broadcasted_iota(jnp.int32, (rows, cap), 1).astype(F32)
         near = (slots == to_column(place_row(o, me))).astype(F32).astype(BF16)
@@ -225,32 +220,8 @@
             a = jnp.dot(near, EOUT[o, 0:cap, columns(n)], preferred_element_type=F32)
             b = jnp.dot(far, RET[o, :, columns(n)], preferred_element_type=F32)
             D[o, :, columns(n)] = (near_w * a + far_w * b).astype(BF16)
-            if i > 0:
-                @pl.when(mid == 0)
-                def _():
-                    sum_copy(o, n, half).start()
-
-    stage_a(0)
-    stage_a(1)
-    stage_b(0)
-    stage_a(2)
-
-    @pl.when(mid == 1)
-    def _():
-        stage_a(3)
-
-    stage_b(1)
-    stage_c(0)
-
-    @pl.when(mid == 0)
-    def _():
-        stage_a(3)
-
-    stage_b(2)
-    stage_c(1)
-    stage_b(3)
-    stage_c(2)
-    stage_c(3)
+            if send:
+                sum_copy(o, n, half).start()
 
     def pass_on(base, way, n):
         o = base + half * (last - 2 * base)
@@ -260,14 +231,43 @@
         D[o, :, columns(n)] = total.astype(BF16)
         copy.start()
 
+    stage_a(0)
+    stage_a(1)
+    for copy in own_w:
+        copy.wait()
+    for copy in w_remote:
+        copy.wait_recv()
+
     @pl.when(mid == 1)
     def _():
+        stage_a(2)
+        stage_a(3)
+        for i in (2, 3, 1, 0):
+            stage_b(i)
+        stage_c(2, False)
         each(lambda n: pass_on(2, half, n))
+        stage_c(3, False)
+        stage_c(1, False)
 
         @each
         def _(n):
             pass_on(3, half, n)
             pass_on(0, 1 - half, n)
+
+        stage_c(0, False)
+
+    @pl.when(mid == 0)
+    def _():
+        stage_b(1)
+        stage_c(1, True)
+        stage_a(2)
+        stage_b(2)
+        stage_c(2, True)
+        stage_a(3)
+        stage_b(3)
+        stage_b(0)
+        stage_c(3, True)
+        stage_c(0, False)
 
     @pl.when(mid == 1)
     def _():

time: 172 us -> 153 us (0.89)
  Pallas kernels: 167 us -> 149 us
    pallas_call x1, Pallas kernels: 167 us -> 149 us  [paired(): pl.pallas_call(functools.partial(layer_kernel, cap, tile), out_shape=jax....]
where the time goes in v3:
time: 153 us
  Pallas kernels  149 us (97%)
  other arithmetic  2.29 us (1%)
  local copies, waits for them, and re-layouts  2.16 us (1%)
    pallas_call x1, Pallas kernels, paired(): pl.pallas_call(functools.partial(layer_kernel, cap, tile), out_shape=jax....  149 us

profile of v3, /device:TPU:0, one launch (start us, length us, event | category | flops | bytes accessed | tf_op | source)
XLA Modules:
  0.0 153.2 jit_solution(10688145687863277772)
XLA Ops:
  0.0 0.7 fusion
  0.7 0.3 reduce_window_sum.11
  1.0 0.7 select_reduce_fusion
  1.7 0.6 pad_maximum_fusion.meta
  2.3 148.8 %shard_map.64 = bf16[128,3584]{1,0:T(8,128)(2,1)} custom-call(bf16[128,3584]{1,0:T(8,128)(2,1)} %tokens.1, f32[16,128]{1,0:T(8,128)} %pad_maximum_fusion.meta, bf16[1,3584,512]{2,1,0:T(8,128)(2,1)} %gate_w.1, bf16[1,3584,512]{2,1,0:T(8,128)(2,1)} %up_w.1, bf16[1,512,3584]{2,1,0:T(8,128)(2,1)} %down_w.1), custom_call_target="tpu_custom_call" | custom-call | flops 14092861440 | bytes 22020096 | tf_op jit(solution)/shard_map/pallas_call | solution.py:320
  151.1 2.2 %copy.8 = bf16[128,3584]{1,0:T(8,128)(2,1)} copy(bf16[128,3584]{1,0:T(8,128)(2,1)} %shard_map.64) | data formatting | bytes 1835008
  (2 shorter events, 0.0 us)

commit v4 on v3

--- a/solution.py
+++ b/solution.py
@@ -232,16 +232,18 @@
         copy.start()
 
     stage_a(0)
-    stage_a(1)
-    for copy in own_w:
-        copy.wait()
-    for copy in w_remote:
-        copy.wait_recv()
+    def weights_here():
+        for copy in own_w:
+            copy.wait()
+        for copy in w_remote:
+            copy.wait_recv()
 
     @pl.when(mid == 1)
     def _():
         stage_a(2)
+        stage_a(1)
         stage_a(3)
+        weights_here()
         for i in (2, 3, 1, 0):
             stage_b(i)
         stage_c(2, False)
@@ -258,9 +260,11 @@
 
     @pl.when(mid == 0)
     def _():
+        stage_a(1)
+        weights_here()
         stage_b(1)
+        stage_a(2)
         stage_c(1, True)
-        stage_a(2)
         stage_b(2)
         stage_c(2, True)
         stage_a(3)

time: 153 us -> 151 us (0.987)
  Pallas kernels: 149 us -> 147 us
    pallas_call x1, Pallas kernels: 149 us -> 147 us  [paired(): pl.pallas_call(functools.partial(layer_kernel, cap, tile), out_shape=jax....]
where the time goes in v4:
time: 151 us
  Pallas kernels  147 us (97%)
  other arithmetic  2.29 us (2%)
  local copies, waits for them, and re-layouts  2.16 us (1%)
    pallas_call x1, Pallas kernels, paired(): pl.pallas_call(functools.partial(layer_kernel, cap, tile), out_shape=jax....  147 us

profile of v4, /device:TPU:0, one launch (start us, length us, event | category | flops | bytes accessed | tf_op | source)
XLA Modules:
  0.0 151.2 jit_solution(11288993062520835423)
XLA Ops:
  0.0 0.7 fusion
  0.7 0.3 reduce_window_sum.11
  1.0 0.7 select_reduce_fusion
  1.7 0.6 pad_maximum_fusion.meta
  2.3 146.7 %shard_map.64 = bf16[128,3584]{1,0:T(8,128)(2,1)} custom-call(bf16[128,3584]{1,0:T(8,128)(2,1)} %tokens.1, f32[16,128]{1,0:T(8,128)} %pad_maximum_fusion.meta, bf16[1,3584,512]{2,1,0:T(8,128)(2,1)} %gate_w.1, bf16[1,3584,512]{2,1,0:T(8,128)(2,1)} %up_w.1, bf16[1,512,3584]{2,1,0:T(8,128)(2,1)} %down_w.1), custom_call_target="tpu_custom_call" | custom-call | flops 14092861440 | bytes 22020096 | tf_op jit(solution)/shard_map/pallas_call | solution.py:324
  149.0 2.2 %copy.8 = bf16[128,3584]{1,0:T(8,128)(2,1)} copy(bf16[128,3584]{1,0:T(8,128)(2,1)} %shard_map.64) | data formatting | bytes 1835008
  (2 shorter events, 0.0 us)
